TPU v7x, 32 devices: a whole 2x2x4 slice. The times are simulated.
32 devices in a mesh: gx: 4 (over x, core), gy: 8 (over z, y).
Axes of the slice: x: 2, y: 2, z: 4, core: 2. Of those that a mesh axis runs over, the one named last changes fastest.
Arguments:
- state: float32 [8, 16, 96, 2048], P(None, None, 'gy', 'gx'), may hold values from -6 to 6
- register: float32 [8, 16, 96, 2048], P(None, None, 'gy', 'gx'), may hold values from -6 to 6
- checkpoint: bfloat16 [8, 16, 96, 2048], P(None, None, 'gy', 'gx'), may hold values from -6 to 6
- velocity: float32 [3, 16, 96, 2048], P(None, None, 'gy', 'gx'), may hold values from -4 to 4
- diffusivity: float32 [16, 96, 2048], P(None, 'gy', 'gx'), may hold values from 0.02 to 0.3
Outputs:
- new_state: float32 [8, 16, 96, 2048], P(None, None, 'gy', 'gx')
- new_register: float32 [8, 16, 96, 2048], P(None, None, 'gy', 'gx')
- gram: float32 [2048, 2048], P('gx', 'gy')
All inputs are finite; a program needn't handle non-finite values.
Results may differ from a plain program's by a relative error of at most 0.0003.
Values sent between devices are 32-bit elements; how exact they have to be, the bound alone decides.
A program may use at most 64 MiB of HBM per device.

v0:
```python
import jax
import jax.numpy as jnp
from jax import lax
from jax.sharding import PartitionSpec as P

step_size = 0.3
carry_weight = -5.0 / 9.0
update_weight = 15.0 / 16.0


def with_halo(shard, sides, width):
    for axis, dim in sides:
        size, length = (lax.axis_size(axis), shard.shape[dim])
        up = [(i, (i + 1) % size) for i in range(size)]
        down = [(j, i) for i, j in up]
        last = lax.slice_in_dim(shard, length - width, length, axis=dim)
        leading = lax.slice_in_dim(shard, 0, width, axis=dim)
        before = lax.ppermute(last, axis, up)
        after = lax.ppermute(leading, axis, down)
        shard = jnp.concatenate([before, shard, after], axis=dim)
    return shard


def shifted(extended, axis, length, offset):
    return lax.slice_in_dim(extended, 2 + offset, 2 + offset + length, axis=axis)


def both_diffs(extended, axis, length):
    center = shifted(extended, axis, length, 0)
    plus_one = shifted(extended, axis, length, 1)
    minus_one = shifted(extended, axis, length, -1)
    plus_two = shifted(extended, axis, length, 2)
    minus_two = shifted(extended, axis, length, -2)
    first = (8.0 * (plus_one - minus_one) - (plus_two - minus_two)) / 12.0
    second = (16.0 * (plus_one + minus_one) - (plus_two + minus_two) - 30.0 * center) / 12.0
    return (first, second)


def tile_block(left, right):
    return lax.dot_general(
        left,
        right,
        (((0, 1, 2), (0, 1, 2)), ((), ())),
        preferred_element_type=jnp.float32,
        precision=lax.Precision.HIGHEST,
    )


def on_device(state, register, checkpoint, velocity, diffusivity):
    tile_y = state.shape[2]
    tile_x = state.shape[3]
    ext_x = with_halo(state, (("gx", 3),), 2)
    ext_y = with_halo(state, (("gy", 2),), 2)
    first_x, second_x = both_diffs(ext_x, 3, tile_x)
    first_y, second_y = both_diffs(ext_y, 2, tile_y)
    plus_one = jnp.roll(state, -1, 1)
    minus_one = jnp.roll(state, 1, 1)
    plus_two = jnp.roll(state, -2, 1)
    minus_two = jnp.roll(state, 2, 1)
    first_z = (8.0 * (plus_one - minus_one) - (plus_two - minus_two)) / 12.0
    second_z = (16.0 * (plus_one + minus_one) - (plus_two + minus_two) - 30.0 * state) / 12.0
    advect = velocity[0][None] * first_x + velocity[1][None] * first_y + velocity[2][None] * first_z
    spread = second_x + second_y + second_z
    tendency = -advect + diffusivity[None] * spread
    new_register = carry_weight * register + step_size * tendency
    new_state = state + update_weight * new_register
    change = new_state - checkpoint.astype(jnp.float32)
    rows = tile_block(change, lax.all_gather(change, "gx", axis=3, tiled=True))
    columns = state.shape[0] * state.shape[1] * tile_y * lax.axis_size("gy")
    summed = lax.psum_scatter(rows, "gy", scatter_dimension=1, tiled=True)
    gram = summed / jnp.float32(columns)
    return (new_state, new_register, gram)


def solution(mesh):
    in_specs = (
        P(None, None, "gy", "gx"),
        P(None, None, "gy", "gx"),
        P(None, None, "gy", "gx"),
        P(None, None, "gy", "gx"),
        P(None, "gy", "gx"),
    )
    out_specs = (P(None, None, "gy", "gx"), P(None, None, "gy", "gx"), P("gx", "gy"))
    return jax.shard_map(
        on_device, mesh=mesh, in_specs=in_specs, out_specs=out_specs, check_vma=False
    )
```

profile of v0, /device:TPU:3, one launch (start us, length us, event | category | flops | bytes accessed | tf_op | source)
XLA Modules:
  0.0 262.0 jit_solution(14410762865352905769)
XLA Ops:
  7.2 0.0 all-gather.2.cloned.1.call-start
  7.2 2.4 fusion.6
  9.6 4.3 %collective-permute-start.2 = (f32[8,16,2,512]{3,1,2,0:T(8,128)}, f32[8,16,2,512]{3,1,2,0:T(8,128)}, u32[]{:S(2)}, u32[]{:S(2)}) collective-permute-start(f32[8,16,2,512]{3,1,2,0:T(8,128)} %get-tuple-element.8), channel_id=1, source_target_pairs={{1,0},{2,1},{3,2},{4,3},{5,4},{6,5},{7,6},{0,7},{9,8},{10,9},{11,1... | collective-permute-start | bytes 1572872 | tf_op jit(solution)/shard_map/ppermute | solution.py:19
  13.9 2.8 %fusion.5 = (f32[8,16,12,2]{3,1,2,0:T(8,128)}, f32[8,16,12,2]{3,1,2,0:T(8,128)}) fusion(f32[8,16,12,512]{3,1,2,0:T(8,128)} %param.5), kind=kLoop, calls=%fused_computation.27 | loop fusion | bytes 49152 | tf_op jit(solution)/shard_map/slice | solution.py:17
  16.7 2.4 copy.14
  19.1 1.1 collective-permute-start.1
  20.2 2.4 copy.13
  22.6 1.1 fusion.8
  23.7 3.6 %fusion.7 = (f32[8,15,12,512]{3,1,2,0:T(8,128)}, f32[8,15,12,512]{3,1,2,0:T(8,128)}) fusion(f32[8,16,12,512]{3,1,2,0:T(8,128)S(1)} %copy-done), kind=kLoop, calls=%fused_computation.29 | loop fusion | bytes 11796480 | tf_op jit(solution)/shard_map/jit(_roll_static)/slice | solution.py:56
  27.3 3.5 %fusion.9 = (f32[8,14,12,512]{3,1,2,0:T(8,128)}, f32[8,14,12,512]{3,1,2,0:T(8,128)}) fusion(f32[8,16,12,512]{3,1,2,0:T(8,128)S(1)} %copy-done), kind=kLoop, calls=%fused_computation.31 | loop fusion | bytes 11010048 | tf_op jit(solution)/shard_map/jit(_roll_static)/slice | solution.py:58
  30.9 1.0 multiply_bitcast_fusion.2
  31.9 1.3 fusion.10
  33.2 0.8 broadcast_multiply_fusion.1
  34.0 2.4 copy.9
  36.4 2.4 copy.11
  38.8 1.1 constant_dynamic-update-slice_fusion.3
  39.9 0.9 constant_dynamic-update-slice_fusion.1
  40.9 1.1 constant_dynamic-update-slice_fusion
  42.0 14.6 %convert_subtract_fusion = (f32[8,16,12,512]{3,1,2,0:T(8,128)}, f32[8,16,12,512]{3,1,2,0:T(8,128)}, f32[8,16,12,512]{3,1,2,0:T(8,128)}) fusion(bf16[8,16,12,512]{3,1,2,0:T(8,128)(2,1)} %param.7, f32[8,16,12,512]{3,1,2,0:T(8,128)S(1)} %copy-done, f32[16,12,512]{2,0,1:T(8,128)} %broadcast_multiply_fusion.1, f32[16,12,512]{2,0,1:T(8,128)S(1)} %copy-done.4, ...), kind=kLoop, calls=%fused_computation.16 | loop fusion | flops 41680896 | bytes 44064768 | tf_op jit(solution)/shard_map/sub | solution.py:67
  56.6 0.2 reduce-scatter.2.cloned.1.call-start
  56.9 83.6 %all-gather.2.cloned.1.call-done = f32[8,16,12,2048]{3,1,2,0:T(8,128)} async-done(((f32[8,16,12,512]{3,1,2,0:T(8,128)}), f32[8,16,12,2048]{3,1,2,0:T(8,128)}) %all-gather.2.cloned.1.call-update) | async-done | bytes 12582928 | tf_op jit(solution)/shard_map/all_gather | solution.py:68
  140.5 23.6 %convolution_bitcast_fusion = f32[512,2048]{1,0:T(8,128)} fusion(f32[8,16,12,512]{3,1,2,0:T(8,128)S(1)} %copy-done.1, f32[8,16,12,2048]{3,1,2,0:T(8,128)} %all-gather.2.cloned.1.call-done), kind=kOutput, calls=%fused_computation.4 | convolution fusion | flops 19327352832 | bytes 19922944 | tf_op jit(solution)/shard_map/dot_general | solution.py:40
  164.1 89.2 %reduce-scatter.2.cloned.1.call-done = f32[512,256]{1,0:T(8,128)} async-done(((f32[512,2048]{1,0:T(8,128)}), f32[512,256]{1,0:T(8,128)}) %reduce-scatter.2.cloned.1.call-update) | async-done | bytes 524304 | tf_op jit(solution)/shard_map/reduce_scatter | solution.py:70
  253.3 1.9 broadcast_multiply_fusion
  (24 shorter events, 0.1 us)
Async XLA Ops:
  7.2 15.4 %copy-start = (f32[8,16,12,512]{3,1,2,0:T(8,128)S(1)}, f32[8,16,12,512]{3,1,2,0:T(8,128)}, u32[]{:S(2)}) copy-start(f32[8,16,12,512]{3,1,2,0:T(8,128)} %param.5) | copy-start | bytes 9437188
  7.2 133.3 %all-gather.2.cloned.1.call-start = ((), (), s32[]{:S(2)}) async-start(), calls=%async_computation.1 | async-start | bytes 15728640 | tf_op jit(solution)/shard_map/all_gather | solution.py:68
  9.6 31.2 %collective-permute-start.2 = (f32[8,16,2,512]{3,1,2,0:T(8,128)}, f32[8,16,2,512]{3,1,2,0:T(8,128)}, u32[]{:S(2)}, u32[]{:S(2)}) collective-permute-start(f32[8,16,2,512]{3,1,2,0:T(8,128)} %get-tuple-element.8), channel_id=1, source_target_pairs={{1,0},{2,1},{3,2},{4,3},{5,4},{6,5},{7,6},{0,7},{9,8},{10,9},{11,1... | collective-permute-start | bytes 1572872 | tf_op jit(solution)/shard_map/ppermute | solution.py:19
  13.9 24.9 %collective-permute-start.3 = (f32[8,16,2,512]{3,1,2,0:T(8,128)}, f32[8,16,2,512]{3,1,2,0:T(8,128)}, u32[]{:S(2)}, u32[]{:S(2)}) collective-permute-start(f32[8,16,2,512]{3,1,2,0:T(8,128)} %get-tuple-element.9), channel_id=1, source_target_pairs={{0,1},{1,2},{2,3},{3,4},{4,5},{5,6},{6,7},{7,0},{8,9},{9,10},{10,1... | collective-permute-start | bytes 1572872 | tf_op jit(solution)/shard_map/ppermute | solution.py:18
  19.1 17.3 %collective-permute-start.1 = (f32[8,16,12,2]{1,0,3,2:T(8,128)}, f32[8,16,12,2]{1,0,3,2:T(8,128)}, u32[]{:S(2)}, u32[]{:S(2)}) collective-permute-start(f32[8,16,12,2]{1,0,3,2:T(8,128)} %copy.14), channel_id=1, source_target_pairs={{0,8},{8,16},{16,24},{24,0},{1,9},{9,17},{17,25},{25,1},{2,10},{10... | collective-permute-start | bytes 36872 | tf_op jit(solution)/shard_map/ppermute | solution.py:18
  22.6 11.4 %collective-permute-start = (f32[8,16,12,2]{1,0,3,2:T(8,128)}, f32[8,16,12,2]{1,0,3,2:T(8,128)}, u32[]{:S(2)}, u32[]{:S(2)}) collective-permute-start(f32[8,16,12,2]{1,0,3,2:T(8,128)} %copy.13), channel_id=1, source_target_pairs={{8,0},{16,8},{24,16},{0,24},{9,1},{17,9},{25,17},{1,25},{10,2},{18... | collective-permute-start | bytes 36872 | tf_op jit(solution)/shard_map/ppermute | solution.py:19
  27.3 3.6 %copy-start.5 = (f32[3,16,12,512]{3,1,2,0:T(8,128)S(1)}, f32[3,16,12,512]{3,1,2,0:T(8,128)}, u32[]{:S(2)}) copy-start(f32[3,16,12,512]{3,1,2,0:T(8,128)} %param.8) | copy-start | bytes 3538948
  30.9 2.3 copy-start.7
  39.9 2.1 copy-start.2
  39.9 2.1 copy-start.3
  39.9 2.1 copy-start.4
  39.9 2.1 copy-start.6
  56.6 83.9 %copy-start.1 = (f32[8,16,12,512]{3,1,2,0:T(8,128)S(1)}, f32[8,16,12,512]{3,1,2,0:T(8,128)}, u32[]{:S(2)}) copy-start(f32[8,16,12,512]{3,1,2,0:T(8,128)} %get-tuple-element.3) | copy-start | bytes 9437188
  56.6 196.7 %reduce-scatter.2.cloned.1.call-start = ((), (), s32[]{:S(2)}) async-start(), calls=%async_computation.2 | async-start | bytes 4718592 | tf_op jit(solution)/shard_map/reduce_scatter | solution.py:70
Sparse Core Ops, SparseCore 0:
  56.7 83.6 all-gather.1
  164.2 89.0 reduce-scatter.1
where the time goes:
time: 264 us; the launch traced here: 262 us
  waiting for transfers between devices  173 us (66%)
  local copies, waits for them, and re-layouts  27.5 us (10%)
  matrix products  23.6 us (9%)
  other arithmetic  18.3 us (7%)
  between operations  14.2 us (5%)
  starting transfers between devices  5.64 us (2%)
    reduce_scatter x1, waiting for transfers between devices, on_device(): summed = lax.psum_scatter(rows, 'gy', scatter_dimension=1, tiled=True)  89.2 us
    all_gather x1, waiting for transfers between devices, on_device(): rows = tile_block(change, lax.all_gather(change, 'gx', axis=3, tiled=True))  83.6 us
    dot_general x1, matrix products, tile_block(): lax.dot_general(left, right, (((0, 1, 2), (0, 1, 2)), ((), ())), preferre...  23.6 us
    sub x1, other arithmetic, on_device(): change = new_state - checkpoint.astype(jnp.float32)  14.6 us
    unnamed x20, local copies, waits for them, and re-layouts  6.82 us
  transfers between devices with their start and end apart: 6, of which 2 were waited for; matrix products, arithmetic and copies ran while one was open for 10% of the time, Pallas kernels for 0%

commit v1 on v0

v1 whole, which is shorter than its diff:
```python
import functools

import jax
import jax.numpy as jnp
from jax import lax
from jax.experimental import pallas as pl
from jax.experimental.pallas import tpu as pltpu
from jax.sharding import PartitionSpec as P

step_size = 0.3
carry_weight = -5.0 / 9.0
update_weight = 15.0 / 16.0
LANES = 128
PACK = LANES // 2
MESH = pl.DeviceIdType.MESH
VMEM = pltpu.VMEM
LIMIT = 56 * 2**20


def halo_kernel(gx, gy, state, y_halo, x_halo, y_send, x_send, y_ssem, y_rsem, x_ssem, x_rsem):
    planes, rows, width = state.shape
    me_x, me_y = lax.axis_index("gx"), lax.axis_index("gy")
    x_up, x_down = lax.rem(me_x + 1, gx), lax.rem(me_x + gx - 1, gx)
    y_up, y_down = lax.rem(me_y + 1, gy), lax.rem(me_y + gy - 1, gy)
    barrier = pltpu.get_barrier_semaphore()
    for device in ((x_up, me_y), (x_down, me_y), (me_x, y_up), (me_x, y_down)):
        pl.semaphore_signal(barrier, inc=1, device_id=device, device_id_type=MESH)

    def pack_y(group, _):
        for k in range(4):
            y_send[0, group, 2 * k : 2 * k + 2, :] = state[4 * group + k, 0:2, :]
            y_send[1, group, 2 * k : 2 * k + 2, :] = state[4 * group + k, rows - 2 : rows, :]
        return 0

    lax.fori_loop(0, planes // 4, pack_y, 0)
    pl.semaphore_wait(barrier, 4)
    copies = []
    for side, target in ((0, y_down), (1, y_up)):
        copies.append(
            pltpu.make_async_remote_copy(
                src_ref=y_send.at[side],
                dst_ref=y_halo.at[side],
                send_sem=y_ssem.at[side],
                recv_sem=y_rsem.at[side],
                device_id=(me_x, target),
                device_id_type=MESH,
            )
        )
        copies[-1].start()

    lane = lax.broadcasted_iota(jnp.int32, (rows, LANES), 1) // 2
    for group in range(planes // PACK):

        def pack_x(pos, kept):
            low, high = kept
            plane = group * PACK + pos
            first = pltpu.roll(state[plane, :, 0:LANES], 2 * pos, 1)
            last = pltpu.roll(state[plane, :, width - LANES : width], lax.rem(2 * pos + 2, LANES), 1)
            return (jnp.where(lane == pos, first, low), jnp.where(lane == pos, last, high))

        zero = jnp.zeros((rows, LANES), jnp.float32)
        low, high = lax.fori_loop(0, PACK, pack_x, (zero, zero))
        x_send[0, group, 0:rows, :] = low
        x_send[1, group, 0:rows, :] = high
        x_send[0, group, rows:, :] = jnp.zeros((x_send.shape[2] - rows, LANES), jnp.float32)
        x_send[1, group, rows:, :] = jnp.zeros((x_send.shape[2] - rows, LANES), jnp.float32)
    for side, target in ((0, x_down), (1, x_up)):
        copies.append(
            pltpu.make_async_remote_copy(
                src_ref=x_send.at[side],
                dst_ref=x_halo.at[side],
                send_sem=x_ssem.at[side],
                recv_sem=x_rsem.at[side],
                device_id=(target, me_y),
                device_id_type=MESH,
            )
        )
        copies[-1].start()
    for copy in copies:
        copy.wait()


def halos(state, gx, gy):
    planes, rows, width = state.shape
    tall = -(-rows // 8) * 8
    y_shape, x_shape = (2, planes // 4, 8, width), (2, planes // PACK, tall, LANES)
    return pl.pallas_call(
        functools.partial(halo_kernel, gx, gy),
        out_shape=(jax.ShapeDtypeStruct(y_shape, jnp.float32), jax.ShapeDtypeStruct(x_shape, jnp.float32)),
        in_specs=[pl.BlockSpec(memory_space=VMEM)],
        out_specs=[pl.BlockSpec(memory_space=VMEM)] * 2,
        scratch_shapes=[VMEM(y_shape, jnp.float32), VMEM(x_shape, jnp.float32)] + [pltpu.SemaphoreType.DMA((2,))] * 4,
        compiler_params=pltpu.CompilerParams(collective_id=0, has_side_effects=True, vmem_limit_bytes=LIMIT),
    )(state)


def stencil_kernel(state, register, checkpoint, velocity, diffusivity, y_halo, x_halo, new_state, new_register, change, ext):
    nz, rows, width = state.shape
    pos0 = lax.rem(pl.program_id(0), PACK // nz) * nz
    tall = rows + 4
    whole = width + LANES
    lane = lax.broadcasted_iota(jnp.int32, (x_halo.shape[2], LANES), 1)
    for z in range(nz):
        ext[z, 0:rows, :] = state[z]
        part = 2 * (z % 4)
        ext[z, rows : rows + 2, :] = y_halo[0, z // 4, part : part + 2, :]
        ext[z, rows + 2 : tall, :] = y_halo[1, z // 4, part : part + 2, :]
    for z in range(nz):
        center = state[z]
        high = ext[z]
        pos = pos0 + z
        right = pltpu.roll(x_halo[0, 0], lax.rem(LANES - 2 * pos, LANES), 1)
        left = pltpu.roll(x_halo[1, 0], lax.rem(2 * LANES - 2 - 2 * pos, LANES), 1)
        beside = jnp.where(lane < 2, right, left)[:rows]
        wide = jnp.concatenate([center, beside], axis=1)
        near = []
        far = []
        advect = None
        for d in range(3):
            if d == 0:
                p1, m1, p2, m2 = (pltpu.roll(wide, k, 1)[:, :width] for k in (whole - 1, 1, whole - 2, 2))
            elif d == 1:
                p1, m1, p2, m2 = (pltpu.roll(high, k, 0)[:rows] for k in (tall - 1, 1, tall - 2, 2))
            else:
                p1, m1, p2, m2 = (state[(z + k) % nz] for k in (1, -1, 2, -2))
            term = velocity[d, z] * (8.0 * (p1 - m1) - (p2 - m2))
            advect = term if advect is None else advect + term
            near.append(p1 + m1)
            far.append(p2 + m2)
        spread = 16.0 * (near[0] + near[1] + near[2]) - (far[0] + far[1] + far[2]) - 90.0 * center
        tendency = (diffusivity[z] * spread - advect) * (1.0 / 12.0)
        increment = carry_weight * register[z] + step_size * tendency
        updated = center + update_weight * increment
        new_register[z] = increment
        new_state[z] = updated
        moved = updated - checkpoint[z].astype(jnp.float32)
        for q in range(width // LANES):
            change[q, rows * z : rows * z + rows, :] = moved[:, q * LANES : (q + 1) * LANES]


def stencil(state, register, checkpoint, velocity, diffusivity, y_halo, x_halo):
    planes, rows, width = state.shape
    nz = diffusivity.shape[0]
    nv = planes // nz
    per_group = PACK // nz
    field = pl.BlockSpec((nz, rows, width), lambda v: (v, 0, 0))
    tall = x_halo.shape[2]
    return pl.pallas_call(
        stencil_kernel,
        grid=(nv,),
        out_shape=(
            jax.ShapeDtypeStruct(state.shape, jnp.float32),
            jax.ShapeDtypeStruct(state.shape, jnp.float32),
            jax.ShapeDtypeStruct((width // LANES, planes * rows, LANES), jnp.float32),
        ),
        in_specs=[
            field,
            field,
            field,
            pl.BlockSpec((3, nz, rows, width), lambda v: (0, 0, 0, 0)),
            pl.BlockSpec((nz, rows, width), lambda v: (0, 0, 0)),
            pl.BlockSpec((2, nz // 4, 8, width), lambda v: (0, v, 0, 0)),
            pl.BlockSpec((2, 1, tall, LANES), lambda v: (0, v // per_group, 0, 0)),
        ],
        out_specs=[field, field, pl.BlockSpec((width // LANES, nz * rows, LANES), lambda v: (0, v, 0))],
        scratch_shapes=[VMEM((nz, rows + 4, width), jnp.float32)],
        compiler_params=pltpu.CompilerParams(vmem_limit_bytes=LIMIT),
        cost_estimate=pl.CostEstimate(flops=50 * planes * rows * width, bytes_accessed=28 * planes * rows * width, transcendentals=0),
    )(state, register, checkpoint, velocity, diffusivity, y_halo, x_halo)


def split(value):
    high = value.astype(jnp.bfloat16)
    return high, (value - high.astype(jnp.float32)).astype(jnp.bfloat16)


def gram_kernel(
    total, own, out, held, lhs_high, lhs_low, product, y_out, y_in, kept, z_in,
    core_ssem, core_rsem, x_ssem, x_rsem, pass_ssem, pass_rsem, y_ssem, y_rsem, z_ssem, z_rsem,
):
    chunks, depth, _ = own.shape
    parts = chunks // 2
    width = chunks * LANES
    i, j = lax.axis_index("gx"), lax.axis_index("gy")
    i0, i1 = lax.rem(i, 2), i // 2
    y, z = lax.rem(j, 2), j // 2
    core = (2 * i1 + 1 - i0, j)
    across = (2 * (1 - i1) + i0, j)
    y_partner = (i, 2 * z + 1 - y)
    blocks = [2 * lax.rem(i1 + s // 2, 2) + lax.rem(i0 + s % 2, 2) for s in range(4)]
    barrier = pltpu.get_barrier_semaphore()
    for device in (core, across, y_partner, *((i, 2 * lax.rem(z + k, 4) + y) for k in (1, 2, 3))):
        pl.semaphore_signal(barrier, inc=1, device_id=device, device_id_type=MESH)
    pl.semaphore_wait(barrier, 6)

    def remote(src, dst, send, recv, device):
        return pltpu.make_async_remote_copy(
            src_ref=src, dst_ref=dst, send_sem=send, recv_sem=recv, device_id=device, device_id_type=MESH
        )

    def chunk_of(t):
        return lax.rem(t // parts + 1 + y, 2) * parts + lax.rem(t, parts)

    def x_copy(t):
        q = chunk_of(t)
        return remote(own.at[q], held.at[1, q], x_ssem.at[t], x_rsem.at[t], across)

    def pass_copy(t):
        q = chunk_of(t)
        return remote(held.at[1, q], held.at[2, q], pass_ssem.at[t], pass_rsem.at[t], core)

    def y_copy(s, part):
        return remote(y_out.at[s, part], y_in.at[s, part], y_ssem.at[s, part], y_rsem.at[s, part], y_partner)

    def z_copy(s, part):
        back = lax.rem(z - blocks[s] + 4, 4)
        slot = jnp.maximum(back, 1) - 1
        return remote(
            kept.at[s, part], z_in.at[slot, part], z_ssem.at[s, part], z_rsem.at[slot, part], (i, 2 * blocks[s] + y)
        )

    for t in range(chunks):
        x_copy(t).start()
    to_core = remote(own, held.at[0], core_ssem, core_rsem, core)
    to_core.start()

    def turn(q, _):
        high, low = split(own[q].T)
        rows = pl.ds(pl.multiple_of(q * LANES, LANES), LANES)
        lhs_high[rows, :] = high
        lhs_low[rows, :] = low
        return 0

    lax.fori_loop(0, chunks, turn, 0)

    step = depth // 3 if depth % (3 * LANES) == 0 else depth

    def multiply(left, right):
        for k in range(0, depth, step):
            block = jnp.concatenate([left[k : k + step, :], right[k : k + step, :]], axis=1)
            high, low = split(block)
            mine_high, mine_low = lhs_high[:, k : k + step], lhs_low[:, k : k + step]
            dot = functools.partial(jnp.dot, preferred_element_type=jnp.float32)
            term = dot(mine_high, high) + dot(mine_high, low) + dot(mine_low, high)
            if k == 0:
                product[...] = term
            else:
                product[...] += term

    def chunk_pair(base, t, left, right):
        multiply(left, right)
        part = lax.rem(t, parts)

        @pl.when(t < parts)
        def _():
            for s in range(2):
                y_out[base + s, part] = product[:, s * LANES : (s + 1) * LANES]
                y_copy(base + s, part).start()

        @pl.when(t >= parts)
        def _():
            for s in range(2):
                kept[base + s, part] = product[:, s * LANES : (s + 1) * LANES]

    def forward(base, part):
        for s in (base, base + 1):
            y_copy(s, part).wait_recv()
            kept[s, part] += y_in[s, part]

            @pl.when(blocks[s] != z)
            def _():
                z_copy(s, part).start()

    to_core.wait_recv()

    def near(t, _):
        q = chunk_of(t)
        chunk_pair(0, t, own.at[q], held.at[0, q])
        return 0

    lax.fori_loop(0, chunks, near, 0)

    def far(t, _):
        q = chunk_of(t)
        x_copy(t).wait_recv()
        pass_copy(t).start()

        @pl.when(t == parts)
        def _():
            for part in range(parts):
                forward(0, part)

        pass_copy(t).wait_recv()
        chunk_pair(2, t, held.at[1, q], held.at[2, q])

        @pl.when(t >= parts)
        def _():
            forward(2, t - parts)

        return 0

    lax.fori_loop(0, chunks, far, 0)
    for s in range(4):

        @pl.when(blocks[s] == z)
        def _():
            for part in range(parts):
                out[:, part * LANES : (part + 1) * LANES] = kept[s, part]

    for part in range(parts):
        for slot in range(3):
            remote(kept.at[0, part], z_in.at[slot, part], z_ssem.at[0, part], z_rsem.at[slot, part], core).wait_recv()
        cols = slice(part * LANES, (part + 1) * LANES)
        out[:, cols] = (out[:, cols] + z_in[0, part] + (z_in[1, part] + z_in[2, part])) / jnp.float32(total)
    to_core.wait_send()
    for t in range(chunks):
        x_copy(t).wait_send()
        pass_copy(t).wait_send()
    for s in range(4):
        for part in range(parts):
            y_copy(s, part).wait_send()

            @pl.when(blocks[s] != z)
            def _():
                z_copy(s, part).wait_send()


def gram_blocks(change, total):
    chunks, depth, _ = change.shape
    width = chunks * LANES
    parts = chunks // 2
    tile = (4, parts, width, LANES)
    dma = pltpu.SemaphoreType.DMA
    return pl.pallas_call(
        functools.partial(gram_kernel, total),
        out_shape=jax.ShapeDtypeStruct((width, parts * LANES), jnp.float32),
        in_specs=[pl.BlockSpec(memory_space=VMEM)],
        out_specs=pl.BlockSpec(memory_space=VMEM),
        scratch_shapes=[
            VMEM((3, chunks, depth, LANES), jnp.float32),
            VMEM((width, depth), jnp.bfloat16),
            VMEM((width, depth), jnp.bfloat16),
            VMEM((width, 2 * LANES), jnp.float32),
            VMEM(tile, jnp.float32),
            VMEM(tile, jnp.float32),
            VMEM(tile, jnp.float32),
            VMEM((3, parts, width, LANES), jnp.float32),
            dma, dma,
            dma((chunks,)), dma((chunks,)),
            dma((chunks,)), dma((chunks,)),
            dma((4, parts)), dma((4, parts)),
            dma((4, parts)), dma((3, parts)),
        ],
        compiler_params=pltpu.CompilerParams(collective_id=1, has_side_effects=True, vmem_limit_bytes=LIMIT),
    )(change)


def on_device(state, register, checkpoint, velocity, diffusivity):
    gx, gy = lax.axis_size("gx"), lax.axis_size("gy")
    nv, nz, rows, width = state.shape
    flat = (nv * nz, rows, width)
    planes = state.reshape(flat)
    y_halo, x_halo = halos(planes, gx, gy)
    new_state, new_register, change = stencil(
        planes, register.reshape(flat), checkpoint.reshape(flat), velocity, diffusivity, y_halo, x_halo
    )
    total = nv * nz * rows * gy
    if gx == 4 and gy == 2 * gx and width % (2 * LANES) == 0:
        gram = gram_blocks(change, total)
    else:
        mine = jnp.moveaxis(change, 0, 1).reshape(nv * nz * rows, width)
        block_rows = lax.dot_general(
            mine,
            lax.all_gather(mine, "gx", axis=1, tiled=True),
            (((0,), (0,)), ((), ())),
            preferred_element_type=jnp.float32,
            precision=lax.Precision.HIGHEST,
        )
        gram = lax.psum_scatter(block_rows, "gy", scatter_dimension=1, tiled=True) / jnp.float32(total)
    return (new_state.reshape(state.shape), new_register.reshape(state.shape), gram)


def solution(mesh):
    tiles = P(None, None, "gy", "gx")
    in_specs = (tiles, tiles, tiles, tiles, P(None, "gy", "gx"))
    out_specs = (tiles, tiles, P("gx", "gy"))
    return jax.shard_map(on_device, mesh=mesh, in_specs=in_specs, out_specs=out_specs, check_vma=False)
```

time: 264 us -> 183 us (0.69)
  waiting for transfers between devices: 173 us -> 0 us
  Pallas kernels: 0 us -> 155 us
  matrix products: 23.6 us -> 0 us
  other arithmetic: 18.3 us -> 0 us
  between operations: 14.2 us -> 0.67 us
  starting transfers between devices: 5.64 us -> 0 us
    pallas_call x0 -> x3, Pallas kernels: none -> 155 us  [the longest x1 109 us: gram_blocks(): pl.pallas_call(functools.partial(gram_kernel, total), out_shape=jax.Shape...]
    reduce_scatter x1 -> x0, waiting for transfers between devices: 89.2 us -> none  [on_device(): summed = lax.psum_scatter(rows, 'gy', scatter_dimension=1, tiled=True)]
    all_gather x1 -> x0, waiting for transfers between devices: 83.6 us -> none  [on_device(): rows = tile_block(change, lax.all_gather(change, 'gx', axis=3, tiled=True))]
    dot_general x1 -> x0, matrix products: 23.6 us -> none  [tile_block(): lax.dot_general(left, right, (((0, 1, 2), (0, 1, 2)), ((), ())), preferre...]
    unnamed x20 -> x16, local copies, waits for them, and re-layouts: 6.82 us -> 26.6 us
    slice x6 -> x0, local copies, waits for them, and re-layouts: 14.7 us -> none  [the longest x2 5.19 us: with_halo(): leading = lax.slice_in_dim(shard, 0, width, axis=dim)]
    sub x1 -> x0, other arithmetic: 14.6 us -> none  [on_device(): change = new_state - checkpoint.astype(jnp.float32)]
    ppermute x4 -> x0, starting transfers between devices: 5.38 us -> none  [the longest x2 4.28 us: with_halo(): after = lax.ppermute(leading, axis, down)]
  transfers between devices with their start and end apart: 6 -> 0, of which waited for: 2 -> 0; matrix products, arithmetic and copies ran while one was open for 10% -> 0% of each run, Pallas kernels for 0% -> 0%
where the time goes in v1:
time: 183 us
  Pallas kernels  155 us (85%)
  local copies, waits for them, and re-layouts  26.6 us (15%)
    pallas_call x1, Pallas kernels, gram_blocks(): pl.pallas_call(functools.partial(gram_kernel, total), out_shape=jax.Shape...  109 us
    pallas_call x1, Pallas kernels, halos(): pl.pallas_call(functools.partial(halo_kernel, gx, gy), out_shape=(jax.Sha...  28.6 us
    unnamed x16, local copies, waits for them, and re-layouts  26.6 us
    pallas_call x1, Pallas kernels, stencil(): pl.pallas_call(stencil_kernel, grid=(nv,), out_shape=(jax.ShapeDtypeStruc...  17.6 us

profile of v1, /device:TPU:3, one launch (start us, length us, event | category | flops | bytes accessed | tf_op | source)
XLA Modules:
  0.0 182.7 jit_solution(2799477761363613619)
XLA Ops:
  0.6 0.0 copy-start.3
  0.6 2.1 %copy.12.diffusivity = f32[16,12,512]{2,1,0:T(8,128)} copy(f32[16,12,512]{2,0,1:T(8,128)} %param.9) | data formatting | bytes 786432 | tf_op args[4]
  2.8 0.0 copy-start.1
  2.8 3.3 %copy.11.velocity = f32[3,16,12,512]{3,2,1,0:T(8,128)} copy(f32[3,16,12,512]{3,1,2,0:T(8,128)} %param.8) | data formatting | bytes 2359296 | tf_op args[3]
  6.1 0.0 copy-done.3
  6.1 2.3 %copy.10 = bf16[8,16,12,512]{3,2,1,0:T(8,128)(2,1)} copy(bf16[8,16,12,512]{3,1,2,0:T(8,128)(2,1)S(1)} %copy-done.3) | data formatting | bytes 3145728 | tf_op args[2]
  8.4 0.0 copy-done.1
  8.4 3.8 %copy.8 = f32[8,16,12,512]{3,2,1,0:T(8,128)} copy(f32[8,16,12,512]{3,1,2,0:T(8,128)S(1)} %copy-done.1) | data formatting | bytes 6291456 | tf_op args[0]
  12.1 0.0 copy-start.2
  12.1 28.6 %shard_map.76 = (f32[2,32,8,512]{3,2,1,0:T(8,128)}, f32[2,2,16,128]{3,2,1,0:T(8,128)}) custom-call(f32[128,12,512]{2,1,0:T(8,128)} %bitcast.5), custom_call_target="tpu_custom_call" | custom-call | tf_op jit(solution)/shard_map/pallas_call | solution.py:87
  40.7 0.0 copy-done.2
  40.7 3.9 %copy.9 = f32[8,16,12,512]{3,2,1,0:T(8,128)} copy(f32[8,16,12,512]{3,1,2,0:T(8,128)S(1)} %copy-done.2) | data formatting | bytes 6291456 | tf_op args[1]
  44.6 17.6 %shard_map.77 = (f32[128,12,512]{2,1,0:T(8,128)}, f32[128,12,512]{2,1,0:T(8,128)}, f32[4,1536,128]{2,1,0:T(8,128)}) custom-call(f32[128,12,512]{2,1,0:T(8,128)} %bitcast.6, f32[128,12,512]{2,1,0:T(8,128)} %bitcast.7, bf16[128,12,512]{2,1,0:T(8,128)(2,1)} %bitcast.8, f32[3,16,12,512]{3,2,1,0:T(8,128)} %copy.11.velocity, f32[16,12,512]{2,1,0:T(8,128)} %copy.12.diffusivity, ...), custom_call_target="tpu_custom_call" | custom-call | flops 39321600 | bytes 22020096 | tf_op jit(solution)/shard_map/pallas_call | solution.py:148
  62.2 0.0 copy-start
  62.2 5.9 %copy.13 = f32[8,16,12,512]{3,1,2,0:T(8,128)} copy(f32[8,16,12,512]{3,2,1,0:T(8,128)} %bitcast.10) | data formatting | bytes 6291456
  68.0 0.0 copy-done
  68.0 3.4 %copy.14 = f32[8,16,12,512]{3,1,2,0:T(8,128)} copy(f32[8,16,12,512]{3,2,1,0:T(8,128)S(1)} %bitcast.9) | data formatting | bytes 6291456
  71.5 109.3 %shard_map.78 = f32[512,256]{1,0:T(8,128)} custom-call(f32[4,1536,128]{2,1,0:T(8,128)} %get-tuple-element.12.own), custom_call_target="tpu_custom_call" | custom-call | tf_op jit(solution)/shard_map/pallas_call | solution.py:334
  180.8 1.9 %copy.16 = f32[512,256]{1,0:T(8,128)} copy(f32[512,256]{1,0:T(8,128)} %shard_map.78) | data formatting | bytes 1048576
Async XLA Ops:
  0.6 5.4 %copy-start.3 = (bf16[8,16,12,512]{3,1,2,0:T(8,128)(2,1)S(1)}, bf16[8,16,12,512]{3,1,2,0:T(8,128)(2,1)}, u32[]{:S(2)}) copy-start(bf16[8,16,12,512]{3,1,2,0:T(8,128)(2,1)} %param.7) | copy-start | bytes 4718596
  2.8 5.6 %copy-start.1 = (f32[8,16,12,512]{3,1,2,0:T(8,128)S(1)}, f32[8,16,12,512]{3,1,2,0:T(8,128)}, u32[]{:S(2)}) copy-start(f32[8,16,12,512]{3,1,2,0:T(8,128)} %param.5) | copy-start | bytes 9437188
  12.1 28.6 %copy-start.2 = (f32[8,16,12,512]{3,1,2,0:T(8,128)S(1)}, f32[8,16,12,512]{3,1,2,0:T(8,128)}, u32[]{:S(2)}) copy-start(f32[8,16,12,512]{3,1,2,0:T(8,128)} %param.6) | copy-start | bytes 9437188
  62.2 5.9 %copy-start = (f32[128,12,512]{2,1,0:T(8,128)S(1)}, f32[128,12,512]{2,1,0:T(8,128)}, u32[]{:S(2)}) copy-start(f32[128,12,512]{2,1,0:T(8,128)} %get-tuple-element.11) | copy-start | bytes 9437188

commit v2 on v1

--- a/solution.py
+++ b/solution.py
@@ -11,34 +11,42 @@
 carry_weight = -5.0 / 9.0
 update_weight = 15.0 / 16.0
 LANES = 128
-PACK = LANES // 2
 MESH = pl.DeviceIdType.MESH
 VMEM = pltpu.VMEM
 LIMIT = 56 * 2**20
 
 
-def halo_kernel(gx, gy, state, y_halo, x_halo, y_send, x_send, y_ssem, y_rsem, x_ssem, x_rsem):
-    planes, rows, width = state.shape
+def pack_columns(state, v, x_send):
+    _, rows, nz, width = state.shape
+    lane = lax.broadcasted_iota(jnp.int32, (nz, LANES), 1) // 2
+    low = jnp.zeros((nz, LANES), jnp.float32)
+    high = low
+    for y in range(rows):
+        first = state[v, y, :, 0:LANES]
+        last = pltpu.roll(state[v, y, :, width - LANES : width], (2 * y + 2) % LANES, 1)
+        low = jnp.where(lane == y, pltpu.roll(first, 2 * y, 1) if y else first, low)
+        high = jnp.where(lane == y, last, high)
+    x_send[0, v] = low
+    x_send[1, v] = high
+
+
+def beside_columns(from_right, from_left, y):
+    lane = lax.broadcasted_iota(jnp.int32, from_right.shape, 1)
+    right = pltpu.roll(from_right, LANES - 2 * y, 1) if y else from_right
+    left = pltpu.roll(from_left, (2 * LANES - 2 - 2 * y) % LANES, 1)
+    return jnp.where(lane < 2, right, left)
+
+
+def halo_copies(gx, gy, state, y_halo, x_send, x_halo, y_ssem, y_rsem, x_ssem, x_rsem):
+    rows = state.shape[1]
     me_x, me_y = lax.axis_index("gx"), lax.axis_index("gy")
     x_up, x_down = lax.rem(me_x + 1, gx), lax.rem(me_x + gx - 1, gx)
     y_up, y_down = lax.rem(me_y + 1, gy), lax.rem(me_y + gy - 1, gy)
-    barrier = pltpu.get_barrier_semaphore()
-    for device in ((x_up, me_y), (x_down, me_y), (me_x, y_up), (me_x, y_down)):
-        pl.semaphore_signal(barrier, inc=1, device_id=device, device_id_type=MESH)
-
-    def pack_y(group, _):
-        for k in range(4):
-            y_send[0, group, 2 * k : 2 * k + 2, :] = state[4 * group + k, 0:2, :]
-            y_send[1, group, 2 * k : 2 * k + 2, :] = state[4 * group + k, rows - 2 : rows, :]
-        return 0
-
-    lax.fori_loop(0, planes // 4, pack_y, 0)
-    pl.semaphore_wait(barrier, 4)
-    copies = []
-    for side, target in ((0, y_down), (1, y_up)):
-        copies.append(
+    along_x, along_y = [], []
+    for side, target, at in ((0, y_down, 0), (1, y_up, rows - 2)):
+        along_y.append(
             pltpu.make_async_remote_copy(
-                src_ref=y_send.at[side],
+                src_ref=state.at[:, at : at + 2],
                 dst_ref=y_halo.at[side],
                 send_sem=y_ssem.at[side],
                 recv_sem=y_rsem.at[side],
@@ -46,26 +54,8 @@
                 device_id_type=MESH,
             )
         )
-        copies[-1].start()
-
-    lane = lax.broadcasted_iota(jnp.int32, (rows, LANES), 1) // 2
-    for group in range(planes // PACK):
-
-        def pack_x(pos, kept):
-            low, high = kept
-            plane = group * PACK + pos
-            first = pltpu.roll(state[plane, :, 0:LANES], 2 * pos, 1)
-            last = pltpu.roll(state[plane, :, width - LANES : width], lax.rem(2 * pos + 2, LANES), 1)
-            return (jnp.where(lane == pos, first, low), jnp.where(lane == pos, last, high))
-
-        zero = jnp.zeros((rows, LANES), jnp.float32)
-        low, high = lax.fori_loop(0, PACK, pack_x, (zero, zero))
-        x_send[0, group, 0:rows, :] = low
-        x_send[1, group, 0:rows, :] = high
-        x_send[0, group, rows:, :] = jnp.zeros((x_send.shape[2] - rows, LANES), jnp.float32)
-        x_send[1, group, rows:, :] = jnp.zeros((x_send.shape[2] - rows, LANES), jnp.float32)
     for side, target in ((0, x_down), (1, x_up)):
-        copies.append(
+        along_x.append(
             pltpu.make_async_remote_copy(
                 src_ref=x_send.at[side],
                 dst_ref=x_halo.at[side],
@@ -75,97 +65,103 @@
                 device_id_type=MESH,
             )
         )
-        copies[-1].start()
-    for copy in copies:
+    return along_x, along_y, ((x_up, me_y), (x_down, me_y), (me_x, y_up), (me_x, y_down))
+
+
+def halo_kernel(gx, gy, state, y_halo, x_halo, x_send, y_ssem, y_rsem, x_ssem, x_rsem):
+    along_x, along_y, near = halo_copies(gx, gy, state, y_halo, x_send, x_halo, y_ssem, y_rsem, x_ssem, x_rsem)
+    barrier = pltpu.get_barrier_semaphore()
+    for device in near:
+        pl.semaphore_signal(barrier, inc=1, device_id=device, device_id_type=MESH)
+    for v in range(state.shape[0]):
+        pack_columns(state, v, x_send)
+    pl.semaphore_wait(barrier, 4)
+    for copy in along_x + along_y:
+        copy.start()
+    for copy in along_x + along_y:
         copy.wait()
 
 
 def halos(state, gx, gy):
-    planes, rows, width = state.shape
-    tall = -(-rows // 8) * 8
-    y_shape, x_shape = (2, planes // 4, 8, width), (2, planes // PACK, tall, LANES)
+    nv, _, nz, width = state.shape
+    y_shape, x_shape = (2, nv, 2, nz, width), (2, nv, nz, LANES)
     return pl.pallas_call(
         functools.partial(halo_kernel, gx, gy),
         out_shape=(jax.ShapeDtypeStruct(y_shape, jnp.float32), jax.ShapeDtypeStruct(x_shape, jnp.float32)),
         in_specs=[pl.BlockSpec(memory_space=VMEM)],
         out_specs=[pl.BlockSpec(memory_space=VMEM)] * 2,
-        scratch_shapes=[VMEM(y_shape, jnp.float32), VMEM(x_shape, jnp.float32)] + [pltpu.SemaphoreType.DMA((2,))] * 4,
+        scratch_shapes=[VMEM(x_shape, jnp.float32)] + [pltpu.SemaphoreType.DMA((2,))] * 4,
         compiler_params=pltpu.CompilerParams(collective_id=0, has_side_effects=True, vmem_limit_bytes=LIMIT),
     )(state)
 
 
-def stencil_kernel(state, register, checkpoint, velocity, diffusivity, y_halo, x_halo, new_state, new_register, change, ext):
-    nz, rows, width = state.shape
-    pos0 = lax.rem(pl.program_id(0), PACK // nz) * nz
-    tall = rows + 4
+def advance(center, beside, around, register, checkpoint, speeds, spreading):
+    nz, width = center.shape
     whole = width + LANES
-    lane = lax.broadcasted_iota(jnp.int32, (x_halo.shape[2], LANES), 1)
-    for z in range(nz):
-        ext[z, 0:rows, :] = state[z]
-        part = 2 * (z % 4)
-        ext[z, rows : rows + 2, :] = y_halo[0, z // 4, part : part + 2, :]
-        ext[z, rows + 2 : tall, :] = y_halo[1, z // 4, part : part + 2, :]
-    for z in range(nz):
-        center = state[z]
-        high = ext[z]
-        pos = pos0 + z
-        right = pltpu.roll(x_halo[0, 0], lax.rem(LANES - 2 * pos, LANES), 1)
-        left = pltpu.roll(x_halo[1, 0], lax.rem(2 * LANES - 2 - 2 * pos, LANES), 1)
-        beside = jnp.where(lane < 2, right, left)[:rows]
-        wide = jnp.concatenate([center, beside], axis=1)
-        near = []
-        far = []
-        advect = None
-        for d in range(3):
-            if d == 0:
-                p1, m1, p2, m2 = (pltpu.roll(wide, k, 1)[:, :width] for k in (whole - 1, 1, whole - 2, 2))
-            elif d == 1:
-                p1, m1, p2, m2 = (pltpu.roll(high, k, 0)[:rows] for k in (tall - 1, 1, tall - 2, 2))
-            else:
-                p1, m1, p2, m2 = (state[(z + k) % nz] for k in (1, -1, 2, -2))
-            term = velocity[d, z] * (8.0 * (p1 - m1) - (p2 - m2))
-            advect = term if advect is None else advect + term
-            near.append(p1 + m1)
-            far.append(p2 + m2)
-        spread = 16.0 * (near[0] + near[1] + near[2]) - (far[0] + far[1] + far[2]) - 90.0 * center
-        tendency = (diffusivity[z] * spread - advect) * (1.0 / 12.0)
-        increment = carry_weight * register[z] + step_size * tendency
-        updated = center + update_weight * increment
-        new_register[z] = increment
-        new_state[z] = updated
-        moved = updated - checkpoint[z].astype(jnp.float32)
+    wide = jnp.concatenate([center, beside], axis=1)
+    along_x = [pltpu.roll(wide, k, 1)[:, :width] for k in (whole - 1, 1, whole - 2, 2)]
+    along_z = [pltpu.roll(center, k, 0) for k in (nz - 1, 1, nz - 2, 2)]
+    advect = near = far = None
+    for speed, (p1, m1, p2, m2) in zip(speeds, (along_x, around, along_z)):
+        term = speed * (8.0 * (p1 - m1) - (p2 - m2))
+        advect = term if advect is None else advect + term
+        near = p1 + m1 if near is None else near + (p1 + m1)
+        far = p2 + m2 if far is None else far + (p2 + m2)
+    spread = 16.0 * near - far - 90.0 * center
+    tendency = (spreading * spread - advect) * (1.0 / 12.0)
+    increment = carry_weight * register + step_size * tendency
+    updated = center + update_weight * increment
+    return updated, increment, updated - checkpoint.astype(jnp.float32)
+
+
+def stencil_kernel(state, register, checkpoint, velocity, diffusivity, y_halo, x_halo, new_state, new_register, change):
+    _, rows, nz, width = state.shape
+
+    def plane(y):
+        if y < 0:
+            return y_halo[1, 0, y + 2]
+        return y_halo[0, 0, y - rows] if y >= rows else state[0, y]
+
+    for y in range(rows):
+        updated, increment, moved = advance(
+            plane(y),
+            beside_columns(x_halo[0, 0], x_halo[1, 0], y),
+            [plane(y + k) for k in (1, -1, 2, -2)],
+            register[0, y],
+            checkpoint[0, y],
+            [velocity[d, y] for d in range(3)],
+            diffusivity[y],
+        )
+        new_register[0, y] = increment
+        new_state[0, y] = updated
         for q in range(width // LANES):
-            change[q, rows * z : rows * z + rows, :] = moved[:, q * LANES : (q + 1) * LANES]
+            change[q, nz * y : nz * y + nz, :] = moved[:, q * LANES : (q + 1) * LANES]
 
 
 def stencil(state, register, checkpoint, velocity, diffusivity, y_halo, x_halo):
-    planes, rows, width = state.shape
-    nz = diffusivity.shape[0]
-    nv = planes // nz
-    per_group = PACK // nz
-    field = pl.BlockSpec((nz, rows, width), lambda v: (v, 0, 0))
-    tall = x_halo.shape[2]
+    nv, rows, nz, width = state.shape
+    cells = nv * rows * nz * width
+    field = pl.BlockSpec((1, rows, nz, width), lambda v: (v, 0, 0, 0))
     return pl.pallas_call(
         stencil_kernel,
         grid=(nv,),
         out_shape=(
             jax.ShapeDtypeStruct(state.shape, jnp.float32),
             jax.ShapeDtypeStruct(state.shape, jnp.float32),
-            jax.ShapeDtypeStruct((width // LANES, planes * rows, LANES), jnp.float32),
+            jax.ShapeDtypeStruct((width // LANES, nv * rows * nz, LANES), jnp.float32),
         ),
         in_specs=[
             field,
             field,
             field,
-            pl.BlockSpec((3, nz, rows, width), lambda v: (0, 0, 0, 0)),
-            pl.BlockSpec((nz, rows, width), lambda v: (0, 0, 0)),
-            pl.BlockSpec((2, nz // 4, 8, width), lambda v: (0, v, 0, 0)),
-            pl.BlockSpec((2, 1, tall, LANES), lambda v: (0, v // per_group, 0, 0)),
+            pl.BlockSpec((3, rows, nz, width), lambda v: (0, 0, 0, 0)),
+            pl.BlockSpec((rows, nz, width), lambda v: (0, 0, 0)),
+            pl.BlockSpec((2, 1, 2, nz, width), lambda v: (0, v, 0, 0, 0)),
+            pl.BlockSpec((2, 1, nz, LANES), lambda v: (0, v, 0, 0)),
         ],
-        out_specs=[field, field, pl.BlockSpec((width // LANES, nz * rows, LANES), lambda v: (0, v, 0))],
-        scratch_shapes=[VMEM((nz, rows + 4, width), jnp.float32)],
+        out_specs=[field, field, pl.BlockSpec((width // LANES, rows * nz, LANES), lambda v: (0, v, 0))],
         compiler_params=pltpu.CompilerParams(vmem_limit_bytes=LIMIT),
-        cost_estimate=pl.CostEstimate(flops=50 * planes * rows * width, bytes_accessed=28 * planes * rows * width, transcendentals=0),
+        cost_estimate=pl.CostEstimate(flops=50 * cells, bytes_accessed=28 * cells, transcendentals=0),
     )(state, register, checkpoint, velocity, diffusivity, y_halo, x_halo)
 
 
@@ -358,11 +354,17 @@
 def on_device(state, register, checkpoint, velocity, diffusivity):
     gx, gy = lax.axis_size("gx"), lax.axis_size("gy")
     nv, nz, rows, width = state.shape
-    flat = (nv * nz, rows, width)
-    planes = state.reshape(flat)
+    by_plane = functools.partial(jnp.swapaxes, axis1=1, axis2=2)
+    planes = by_plane(state)
     y_halo, x_halo = halos(planes, gx, gy)
     new_state, new_register, change = stencil(
-        planes, register.reshape(flat), checkpoint.reshape(flat), velocity, diffusivity, y_halo, x_halo
+        planes,
+        by_plane(register),
+        by_plane(checkpoint),
+        by_plane(velocity),
+        jnp.swapaxes(diffusivity, 0, 1),
+        y_halo,
+        x_halo,
     )
     total = nv * nz * rows * gy
     if gx == 4 and gy == 2 * gx and width % (2 * LANES) == 0:
@@ -377,7 +379,7 @@
             precision=lax.Precision.HIGHEST,
         )
         gram = lax.psum_scatter(block_rows, "gy", scatter_dimension=1, tiled=True) / jnp.float32(total)
-    return (new_state.reshape(state.shape), new_register.reshape(state.shape), gram)
+    return (by_plane(new_state), by_plane(new_register), gram)
 
 
 def solution(mesh):

time: 183 us -> 155 us (0.85)
  local copies, waits for them, and re-layouts: 26.6 us -> 1.87 us
  Pallas kernels: 155 us -> 152 us
    unnamed x16 -> x1, local copies, waits for them, and re-layouts: 26.6 us -> 1.87 us
    pallas_call x1, Pallas kernels: 17.6 us -> 14.4 us  [stencil(): pl.pallas_call(stencil_kernel, grid=(nv,), out_shape=(jax.ShapeDtypeStruc...]
where the time goes in v2:
time: 155 us; the launch traced here: 154 us
  Pallas kernels  152 us (98%)
  local copies, waits for them, and re-layouts  1.87 us (1%)
    pallas_call x1, Pallas kernels, gram_blocks(): pl.pallas_call(functools.partial(gram_kernel, total), out_shape=jax.Shape...  109 us
    pallas_call x1, Pallas kernels, halos(): pl.pallas_call(functools.partial(halo_kernel, gx, gy), out_shape=(jax.Sha...  28.1 us
    pallas_call x1, Pallas kernels, stencil(): pl.pallas_call(stencil_kernel, grid=(nv,), out_shape=(jax.ShapeDtypeStruc...  14.4 us

profile of v2, /device:TPU:3, one launch (start us, length us, event | category | flops | bytes accessed | tf_op | source)
XLA Modules:
  0.0 154.4 jit_solution(11645776182405284658)
XLA Ops:
  0.6 28.1 %shard_map.76 = (f32[2,8,2,16,512]{4,3,2,1,0:T(8,128)}, f32[2,8,16,128]{3,2,1,0:T(8,128)}) custom-call(f32[8,12,16,512]{3,2,1,0:T(8,128)} %bitcast.7), custom_call_target="tpu_custom_call" | custom-call | tf_op jit(solution)/shard_map/pallas_call | solution.py:88
  28.8 14.4 %shard_map.77 = (f32[8,12,16,512]{3,2,1,0:T(8,128)}, f32[8,12,16,512]{3,2,1,0:T(8,128)}, f32[4,1536,128]{2,1,0:T(8,128)}) custom-call(f32[8,12,16,512]{3,2,1,0:T(8,128)} %bitcast.8, f32[8,12,16,512]{3,2,1,0:T(8,128)} %bitcast.9, bf16[8,12,16,512]{3,2,1,0:T(8,128)(2,1)} %bitcast.10, f32[3,12,16,512]{3,2,1,0:T(8,128)} %bitcast.11, f32[12,16,512]{2,1,0:T(8,128)} %bitcast.12, ...), custom_call_target="tpu_custom_call" | custom-call | flops 39321600 | bytes 22020096 | tf_op jit(solution)/shard_map/pallas_call | solution.py:145
  43.2 109.4 %shard_map.78 = f32[512,256]{1,0:T(8,128)} custom-call(f32[4,1536,128]{2,1,0:T(8,128)} %get-tuple-element.12.own), custom_call_target="tpu_custom_call" | custom-call | tf_op jit(solution)/shard_map/pallas_call | solution.py:330
  152.6 1.9 %copy.9 = f32[512,256]{1,0:T(8,128)} copy(f32[512,256]{1,0:T(8,128)} %shard_map.78) | data formatting | bytes 1048576

commit v3 on v2

--- a/solution.py
+++ b/solution.py
@@ -170,13 +170,18 @@
     return high, (value - high.astype(jnp.float32)).astype(jnp.bfloat16)
 
 
-def gram_kernel(
-    total, own, out, held, lhs_high, lhs_low, product, y_out, y_in, kept, z_in,
+def section_kernel(
+    gx, gy, total, state_in, register_in, checkpoint_in, velocity_in, diffusivity_in, state_out, register_out, out,
+    state, register, checkpoint, velocity, diffusivity, updated, y_halo, x_send, x_halo,
+    own, held, lhs_high, lhs_low, product, y_out, y_in, kept, z_in,
+    load_sem, store_sem, hy_ssem, hy_rsem, hx_ssem, hx_rsem,
     core_ssem, core_rsem, x_ssem, x_rsem, pass_ssem, pass_rsem, y_ssem, y_rsem, z_ssem, z_rsem,
 ):
-    chunks, depth, _ = own.shape
+    nv, rows, nz, width = state.shape
+    chunks = width // LANES
     parts = chunks // 2
-    width = chunks * LANES
+    inner = (rows - 4) * nz
+    bounds = (0, (nv // 2) * inner, nv * inner, nv * rows * nz)
     i, j = lax.axis_index("gx"), lax.axis_index("gy")
     i0, i1 = lax.rem(i, 2), i // 2
     y, z = lax.rem(j, 2), j // 2
@@ -184,10 +189,33 @@
     across = (2 * (1 - i1) + i0, j)
     y_partner = (i, 2 * z + 1 - y)
     blocks = [2 * lax.rem(i1 + s // 2, 2) + lax.rem(i0 + s % 2, 2) for s in range(4)]
+    along_x, along_y, near_by = halo_copies(gx, gy, state, y_halo, x_send, x_halo, hy_ssem, hy_rsem, hx_ssem, hx_rsem)
+    pairs = (
+        (state_in, state),
+        (velocity_in, velocity),
+        (diffusivity_in, diffusivity),
+        (register_in, register),
+        (checkpoint_in, checkpoint),
+    )
+    loads = [pltpu.make_async_copy(src, dst, load_sem.at[n]) for n, (src, dst) in enumerate(pairs)]
+    for load in loads:
+        load.start()
+    greeted = (*near_by, core, across, y_partner, *((i, 2 * lax.rem(z + k, 4) + y) for k in (1, 2, 3)))
     barrier = pltpu.get_barrier_semaphore()
-    for device in (core, across, y_partner, *((i, 2 * lax.rem(z + k, 4) + y) for k in (1, 2, 3))):
+    for device in greeted:
         pl.semaphore_signal(barrier, inc=1, device_id=device, device_id_type=MESH)
-    pl.semaphore_wait(barrier, 6)
+    loads[0].wait()
+    pl.semaphore_wait(barrier, len(greeted))
+    for copy in along_y:
+        copy.start()
+
+    def pack(v, _):
+        pack_columns(state, v, x_send)
+        return 0
+
+    lax.fori_loop(0, nv, pack, 0)
+    for copy in along_x:
+        copy.start()
 
     def remote(src, dst, send, recv, device):
         return pltpu.make_async_remote_copy(
@@ -197,13 +225,19 @@
     def chunk_of(t):
         return lax.rem(t // parts + 1 + y, 2) * parts + lax.rem(t, parts)
 
-    def x_copy(t):
+    def span(k):
+        return pl.ds(bounds[k], bounds[k + 1] - bounds[k])
+
+    def x_copy(k, t):
         q = chunk_of(t)
-        return remote(own.at[q], held.at[1, q], x_ssem.at[t], x_rsem.at[t], across)
-
-    def pass_copy(t):
+        return remote(own.at[q, span(k)], held.at[1, q, span(k)], x_ssem.at[k, t], x_rsem.at[k, t], across)
+
+    def pass_copy(k, t):
         q = chunk_of(t)
-        return remote(held.at[1, q], held.at[2, q], pass_ssem.at[t], pass_rsem.at[t], core)
+        return remote(held.at[1, q, span(k)], held.at[2, q, span(k)], pass_ssem.at[k, t], pass_rsem.at[k, t], core)
+
+    def core_copy(k):
+        return remote(own.at[:, span(k)], held.at[0, :, span(k)], core_ssem.at[k], core_rsem.at[k], core)
 
     def y_copy(s, part):
         return remote(y_out.at[s, part], y_in.at[s, part], y_ssem.at[s, part], y_rsem.at[s, part], y_partner)
@@ -215,48 +249,67 @@
             kept.at[s, part], z_in.at[slot, part], z_ssem.at[s, part], z_rsem.at[slot, part], (i, 2 * blocks[s] + y)
         )
 
-    for t in range(chunks):
-        x_copy(t).start()
-    to_core = remote(own, held.at[0], core_ssem, core_rsem, core)
-    to_core.start()
-
-    def turn(q, _):
-        high, low = split(own[q].T)
-        rows = pl.ds(pl.multiple_of(q * LANES, LANES), LANES)
-        lhs_high[rows, :] = high
-        lhs_low[rows, :] = low
-        return 0
-
-    lax.fori_loop(0, chunks, turn, 0)
-
-    step = depth // 3 if depth % (3 * LANES) == 0 else depth
-
-    def multiply(left, right):
-        for k in range(0, depth, step):
-            block = jnp.concatenate([left[k : k + step, :], right[k : k + step, :]], axis=1)
-            high, low = split(block)
-            mine_high, mine_low = lhs_high[:, k : k + step], lhs_low[:, k : k + step]
-            dot = functools.partial(jnp.dot, preferred_element_type=jnp.float32)
-            term = dot(mine_high, high) + dot(mine_high, low) + dot(mine_low, high)
-            if k == 0:
-                product[...] = term
-            else:
-                product[...] += term
-
-    def chunk_pair(base, t, left, right):
-        multiply(left, right)
+    def compute(v, which, base):
+        def plane(at):
+            if at < 0:
+                return y_halo[1, v, at + 2]
+            return y_halo[0, v, at - rows] if at >= rows else state[v, at]
+
+        for n, at in enumerate(which):
+            fresh, increment, moved = advance(
+                plane(at),
+                beside_columns(x_halo[0, v], x_halo[1, v], at),
+                [plane(at + k) for k in (1, -1, 2, -2)],
+                register[v, at],
+                checkpoint[v, at],
+                [velocity[d, at] for d in range(3)],
+                diffusivity[at],
+            )
+            register[v, at] = increment
+            updated[v, at] = fresh
+            place = pl.ds(pl.multiple_of(base + n * nz, nz), nz)
+            for q in range(chunks):
+                own[q, place, :] = moved[:, q * LANES : (q + 1) * LANES]
+
+    def send(k):
+        for t in range(chunks):
+            x_copy(k, t).start()
+        core_copy(k).start()
+
+    def turn(k):
+        def one(q, _):
+            high, low = split(own[q, bounds[k] : bounds[k + 1], :].T)
+            place = pl.ds(pl.multiple_of(q * LANES, LANES), LANES)
+            lhs_high[place, bounds[k] : bounds[k + 1]] = high
+            lhs_low[place, bounds[k] : bounds[k + 1]] = low
+            return 0
+
+        lax.fori_loop(0, chunks, one, 0)
+
+    def multiply(t, left, right, k):
+        block = jnp.concatenate([left[bounds[k] : bounds[k + 1], :], right[bounds[k] : bounds[k + 1], :]], axis=1)
+        high, low = split(block)
+        mine_high, mine_low = lhs_high[:, bounds[k] : bounds[k + 1]], lhs_low[:, bounds[k] : bounds[k + 1]]
+        dot = functools.partial(jnp.dot, preferred_element_type=jnp.float32)
+        term = dot(mine_high, high) + dot(mine_high, low) + dot(mine_low, high)
+        if k == 0:
+            product[t] = term
+        else:
+            product[t] += term
+
+    def deal(base, t):
         part = lax.rem(t, parts)
 
         @pl.when(t < parts)
         def _():
             for s in range(2):
-                y_out[base + s, part] = product[:, s * LANES : (s + 1) * LANES]
+                y_out[base + s, part] = product[t, :, s * LANES : (s + 1) * LANES]
                 y_copy(base + s, part).start()
 
         @pl.when(t >= parts)
         def _():
             for s in range(2):
-                kept[base + s, part] = product[:, s * LANES : (s + 1) * LANES]
+                kept[base + s, part] = product[t, :, s * LANES : (s + 1) * LANES]
 
     def forward(base, part):
         for s in (base, base + 1):
@@ -267,27 +320,73 @@
             def _():
                 z_copy(s, part).start()
 
-    to_core.wait_recv()
+    for load in loads[1:]:
+        load.wait()
+    for copy in along_x:
+        copy.wait_recv()
+    for k in range(2):
+
+        def inside(v, _):
+            compute(v, range(2, rows - 2), v * inner)
+            return 0
+
+        lax.fori_loop((0, nv // 2)[k], (nv // 2, nv)[k], inside, 0)
+        send(k)
+    for k in range(2):
+        turn(k)
+    for copy in along_y:
+        copy.wait_recv()
+
+    def outside(v, _):
+        compute(v, (0, 1, rows - 2, rows - 1), bounds[2] + v * 4 * nz)
+        return 0
+
+    lax.fori_loop(0, nv, outside, 0)
+    send(2)
+    stores = [
+        pltpu.make_async_copy(updated, state_out, store_sem.at[0]),
+        pltpu.make_async_copy(register, register_out, store_sem.at[1]),
+    ]
+    for store in stores:
+        store.start()
+    turn(2)
+    for k in range(3):
+        core_copy(k).wait_recv()
 
     def near(t, _):
         q = chunk_of(t)
-        chunk_pair(0, t, own.at[q], held.at[0, q])
+        for k in range(3):
+            multiply(t, own.at[q], held.at[0, q], k)
+        deal(0, t)
         return 0
 
     lax.fori_loop(0, chunks, near, 0)
+    for k in range(2):
+
+        def early(t, _):
+            x_copy(k, t).wait_recv()
+            pass_copy(k, t).start()
+            return 0
+
+        def partial(t, _):
+            q = chunk_of(t)
+            pass_copy(k, t).wait_recv()
+            multiply(t, held.at[1, q], held.at[2, q], k)
+            return 0
+
+        lax.fori_loop(0, chunks, early, 0)
+        lax.fori_loop(0, chunks, partial, 0)
+        if k == 0:
+            for part in range(parts):
+                forward(0, part)
 
     def far(t, _):
         q = chunk_of(t)
-        x_copy(t).wait_recv()
-        pass_copy(t).start()
-
-        @pl.when(t == parts)
-        def _():
-            for part in range(parts):
-                forward(0, part)
-
-        pass_copy(t).wait_recv()
-        chunk_pair(2, t, held.at[1, q], held.at[2, q])
+        x_copy(2, t).wait_recv()
+        pass_copy(2, t).start()
+        pass_copy(2, t).wait_recv()
+        multiply(t, held.at[1, q], held.at[2, q], 2)
+        deal(2, t)
 
         @pl.when(t >= parts)
         def _():
@@ -308,10 +407,15 @@
             remote(kept.at[0, part], z_in.at[slot, part], z_ssem.at[0, part], z_rsem.at[slot, part], core).wait_recv()
         cols = slice(part * LANES, (part + 1) * LANES)
         out[:, cols] = (out[:, cols] + z_in[0, part] + (z_in[1, part] + z_in[2, part])) / jnp.float32(total)
-    to_core.wait_send()
-    for t in range(chunks):
-        x_copy(t).wait_send()
-        pass_copy(t).wait_send()
+    for copy in along_x + along_y:
+        copy.wait_send()
+    for store in stores:
+        store.wait()
+    for k in range(3):
+        core_copy(k).wait_send()
+        for t in range(chunks):
+            x_copy(k, t).wait_send()
+            pass_copy(k, t).wait_send()
     for s in range(4):
         for part in range(parts):
             y_copy(s, part).wait_send()
@@ -321,55 +425,62 @@
                 z_copy(s, part).wait_send()
 
 
-def gram_blocks(change, total):
-    chunks, depth, _ = change.shape
-    width = chunks * LANES
+def whole_section(arrays, gx, gy, total):
+    nv, rows, nz, width = arrays[0].shape
+    chunks = width // LANES
     parts = chunks // 2
+    depth = nv * rows * nz
+    f32 = jnp.float32
     tile = (4, parts, width, LANES)
+    x_shape = (2, nv, nz, LANES)
     dma = pltpu.SemaphoreType.DMA
+    whole = pl.BlockSpec(memory_space=pl.ANY)
     return pl.pallas_call(
-        functools.partial(gram_kernel, total),
-        out_shape=jax.ShapeDtypeStruct((width, parts * LANES), jnp.float32),
-        in_specs=[pl.BlockSpec(memory_space=VMEM)],
-        out_specs=pl.BlockSpec(memory_space=VMEM),
-        scratch_shapes=[
-            VMEM((3, chunks, depth, LANES), jnp.float32),
+        functools.partial(section_kernel, gx, gy, total),
+        out_shape=(
+            jax.ShapeDtypeStruct(arrays[0].shape, f32),
+            jax.ShapeDtypeStruct(arrays[0].shape, f32),
+            jax.ShapeDtypeStruct((width, parts * LANES), f32),
+        ),
+        in_specs=[whole] * 5,
+        out_specs=(whole, whole, pl.BlockSpec(memory_space=VMEM)),
+        scratch_shapes=[VMEM(array.shape, array.dtype) for array in arrays]
+        + [
+            VMEM(arrays[0].shape, f32),
+            VMEM((2, nv, 2, nz, width), f32),
+            VMEM(x_shape, f32),
+            VMEM(x_shape, f32),
+            VMEM((chunks, depth, LANES), f32),
+            VMEM((3, chunks, depth, LANES), f32),
             VMEM((width, depth), jnp.bfloat16),
             VMEM((width, depth), jnp.bfloat16),
-            VMEM((width, 2 * LANES), jnp.float32),
-            VMEM(tile, jnp.float32),
-            VMEM(tile, jnp.float32),
-            VMEM(tile, jnp.float32),
-            VMEM((3, parts, width, LANES), jnp.float32),
-            dma, dma,
-            dma((chunks,)), dma((chunks,)),
-            dma((chunks,)), dma((chunks,)),
+            VMEM((chunks, width, 2 * LANES), f32),
+            VMEM(tile, f32),
+            VMEM(tile, f32),
+            VMEM(tile, f32),
+            VMEM((3, parts, width, LANES), f32),
+            dma((5,)), dma((2,)),
+            dma((2,)), dma((2,)), dma((2,)), dma((2,)),
+            dma((3,)), dma((3,)),
+            dma((3, chunks)), dma((3, chunks)),
+            dma((3, chunks)), dma((3, chunks)),
             dma((4, parts)), dma((4, parts)),
             dma((4, parts)), dma((3, parts)),
         ],
         compiler_params=pltpu.CompilerParams(collective_id=1, has_side_effects=True, vmem_limit_bytes=LIMIT),
-    )(change)
+    )(*arrays)
 
 
 def on_device(state, register, checkpoint, velocity, diffusivity):
     gx, gy = lax.axis_size("gx"), lax.axis_size("gy")
     nv, nz, rows, width = state.shape
     by_plane = functools.partial(jnp.swapaxes, axis1=1, axis2=2)
-    planes = by_plane(state)
-    y_halo, x_halo = halos(planes, gx, gy)
-    new_state, new_register, change = stencil(
-        planes,
-        by_plane(register),
-        by_plane(checkpoint),
-        by_plane(velocity),
-        jnp.swapaxes(diffusivity, 0, 1),
-        y_halo,
-        x_halo,
-    )
+    arrays = [by_plane(a) for a in (state, register, checkpoint, velocity)] + [jnp.swapaxes(diffusivity, 0, 1)]
     total = nv * nz * rows * gy
-    if gx == 4 and gy == 2 * gx and width % (2 * LANES) == 0:
-        gram = gram_blocks(change, total)
+    if gx == 4 and gy == 2 * gx and width % (2 * LANES) == 0 and rows > 4:
+        new_state, new_register, gram = whole_section(arrays, gx, gy, total)
     else:
+        new_state, new_register, change = stencil(*arrays, *halos(arrays[0], gx, gy))
         mine = jnp.moveaxis(change, 0, 1).reshape(nv * nz * rows, width)
         block_rows = lax.dot_general(
             mine,

time: 155 us -> 132 us (0.85)
  Pallas kernels: 152 us -> 124 us
  local copies, waits for them, and re-layouts: 1.87 us -> 6.74 us
    pallas_call x3 -> x1, Pallas kernels: 152 us -> 124 us  [whole_section(): pl.pallas_call(functools.partial(section_kernel, gx, gy, total), out_shap...]
    unnamed x1 -> x7, local copies, waits for them, and re-layouts: 1.87 us -> 6.74 us
where the time goes in v3:
time: 132 us
  Pallas kernels  124 us (94%)
  local copies, waits for them, and re-layouts  6.74 us (5%)
    pallas_call x1, Pallas kernels, whole_section(): pl.pallas_call(functools.partial(section_kernel, gx, gy, total), out_shap...  124 us
    unnamed x7, local copies, waits for them, and re-layouts  6.74 us

profile of v3, /device:TPU:3, one launch (start us, length us, event | category | flops | bytes accessed | tf_op | source)
XLA Modules:
  0.0 131.6 jit_solution(12090809673939978428)
XLA Ops:
  0.6 124.2 %shard_map.76 = (f32[8,12,16,512]{3,2,1,0:T(8,128)}, f32[8,12,16,512]{3,2,1,0:T(8,128)}, f32[512,256]{1,0:T(8,128)}) custom-call(f32[8,12,16,512]{3,2,1,0:T(8,128)} %bitcast.9, f32[8,12,16,512]{3,2,1,0:T(8,128)} %bitcast.10, bf16[8,12,16,512]{3,2,1,0:T(8,128)(2,1)} %bitcast.11, f32[3,12,16,512]{3,2,1,0:T(8,128)} %bitcast.12, f32[12,16,512]{2,1,0:T(8,128)} %bitcast.13), custom_call_target="tpu_custom_call" | custom-call | tf_op jit(solution)/shard_map/pallas_call | solution.py:438
  124.8 0.0 copy-start
  124.8 4.3 %copy.11 = f32[8,16,12,512]{3,1,2,0:T(8,128)} copy(f32[8,16,12,512]{3,1,2,0:T(8,128)} %bitcast.8) | data formatting | bytes 6291456
  129.1 0.0 copy-done
  129.1 0.0 copy-start.1
  129.1 1.7 %copy.12 = f32[8,16,12,512]{3,1,2,0:T(8,128)} copy(f32[8,16,12,512]{3,1,2,0:T(8,128)S(1)} %bitcast.7) | data formatting | bytes 6291456
  130.8 0.0 copy-done.1
  130.8 0.8 copy.13
Async XLA Ops:
  124.8 4.3 %copy-start = (f32[8,12,16,512]{3,2,1,0:T(8,128)S(1)}, f32[8,12,16,512]{3,2,1,0:T(8,128)}, u32[]{:S(2)}) copy-start(f32[8,12,16,512]{3,2,1,0:T(8,128)} %get-tuple-element.7) | copy-start | bytes 9437188
  129.1 1.7 %copy-start.1 = (f32[512,256]{1,0:T(8,128)S(1)}, f32[512,256]{1,0:T(8,128)}, u32[]{:S(2)}) copy-start(f32[512,256]{1,0:T(8,128)} %get-tuple-element.14) | copy-start | bytes 1572868

commit v4 on v3

--- a/solution.py
+++ b/solution.py
@@ -223,7 +223,7 @@
         )
 
     def chunk_of(t):
-        return lax.rem(t // parts + 1 + y, 2) * parts + lax.rem(t, parts)
+        return lax.rem(t + 1 + y, 2) * parts + t // 2
 
     def span(k):
         return pl.ds(bounds[k], bounds[k + 1] - bounds[k])
@@ -271,11 +271,6 @@
             for q in range(chunks):
                 own[q, place, :] = moved[:, q * LANES : (q + 1) * LANES]
 
-    def send(k):
-        for t in range(chunks):
-            x_copy(k, t).start()
-        core_copy(k).start()
-
     def turn(k):
         def one(q, _):
             high, low = split(own[q, bounds[k] : bounds[k + 1], :].T)
@@ -298,15 +293,15 @@
             product[t] += term
 
     def deal(base, t):
-        part = lax.rem(t, parts)
-
-        @pl.when(t < parts)
+        part = t // 2
+
+        @pl.when(lax.rem(t, 2) == 0)
         def _():
             for s in range(2):
                 y_out[base + s, part] = product[t, :, s * LANES : (s + 1) * LANES]
                 y_copy(base + s, part).start()
 
-        @pl.when(t >= parts)
+        @pl.when(lax.rem(t, 2) == 1)
         def _():
             for s in range(2):
                 kept[base + s, part] = product[t, :, s * LANES : (s + 1) * LANES]
@@ -331,7 +326,9 @@
             return 0
 
         lax.fori_loop((0, nv // 2)[k], (nv // 2, nv)[k], inside, 0)
-        send(k)
+        for t in range(1 if k else chunks):
+            x_copy(k, t).start()
+        core_copy(k).start()
     for k in range(2):
         turn(k)
     for copy in along_y:
@@ -342,7 +339,11 @@
         return 0
 
     lax.fori_loop(0, nv, outside, 0)
-    send(2)
+    for t in range(chunks):
+        if t:
+            x_copy(1, t).start()
+        x_copy(2, t).start()
+    core_copy(2).start()
     stores = [
         pltpu.make_async_copy(updated, state_out, store_sem.at[0]),
         pltpu.make_async_copy(register, register_out, store_sem.at[1]),
@@ -361,36 +362,37 @@
         return 0
 
     lax.fori_loop(0, chunks, near, 0)
-    for k in range(2):
-
-        def early(t, _):
+    def early(t, _):
+        x_copy(0, t).wait_recv()
+        pass_copy(0, t).start()
+        return 0
+
+    def partial(t, _):
+        q = chunk_of(t)
+        pass_copy(0, t).wait_recv()
+        multiply(t, held.at[1, q], held.at[2, q], 0)
+        return 0
+
+    lax.fori_loop(0, chunks, early, 0)
+    lax.fori_loop(0, chunks, partial, 0)
+
+    def far(t, _):
+        q = chunk_of(t)
+        for k in (1, 2):
             x_copy(k, t).wait_recv()
             pass_copy(k, t).start()
-            return 0
-
-        def partial(t, _):
-            q = chunk_of(t)
+        for k in (1, 2):
             pass_copy(k, t).wait_recv()
             multiply(t, held.at[1, q], held.at[2, q], k)
-            return 0
-
-        lax.fori_loop(0, chunks, early, 0)
-        lax.fori_loop(0, chunks, partial, 0)
-        if k == 0:
-            for part in range(parts):
-                forward(0, part)
-
-    def far(t, _):
-        q = chunk_of(t)
-        x_copy(2, t).wait_recv()
-        pass_copy(2, t).start()
-        pass_copy(2, t).wait_recv()
-        multiply(t, held.at[1, q], held.at[2, q], 2)
         deal(2, t)
 
-        @pl.when(t >= parts)
+        @pl.when(lax.rem(t, 2) == 0)
         def _():
-            forward(2, t - parts)
+            forward(0, t // 2)
+
+        @pl.when(lax.rem(t, 2) == 1)
+        def _():
+            forward(2, t // 2)
 
         return 0
 

time: 132 us -> 121 us (0.917)
  Pallas kernels: 124 us -> 113 us
    pallas_call x1, Pallas kernels: 124 us -> 113 us  [whole_section(): pl.pallas_call(functools.partial(section_kernel, gx, gy, total), out_shap...]
where the time goes in v4:
time: 121 us; the launch traced here: 120 us
  Pallas kernels  113 us (93%)
  local copies, waits for them, and re-layouts  6.74 us (6%)
    pallas_call x1, Pallas kernels, whole_section(): pl.pallas_call(functools.partial(section_kernel, gx, gy, total), out_shap...  113 us
    unnamed x7, local copies, waits for them, and re-layouts  6.74 us

profile of v4, /device:TPU:3, one launch (start us, length us, event | category | flops | bytes accessed | tf_op | source)
XLA Modules:
  0.0 120.4 jit_solution(12101763256552544097)
XLA Ops:
  0.6 113.0 %shard_map.76 = (f32[8,12,16,512]{3,2,1,0:T(8,128)}, f32[8,12,16,512]{3,2,1,0:T(8,128)}, f32[512,256]{1,0:T(8,128)}) custom-call(f32[8,12,16,512]{3,2,1,0:T(8,128)} %bitcast.9, f32[8,12,16,512]{3,2,1,0:T(8,128)} %bitcast.10, bf16[8,12,16,512]{3,2,1,0:T(8,128)(2,1)} %bitcast.11, f32[3,12,16,512]{3,2,1,0:T(8,128)} %bitcast.12, f32[12,16,512]{2,1,0:T(8,128)} %bitcast.13), custom_call_target="tpu_custom_call" | custom-call | tf_op jit(solution)/shard_map/pallas_call | solution.py:440
  113.7 0.0 copy-start
  113.7 4.3 %copy.11 = f32[8,16,12,512]{3,1,2,0:T(8,128)} copy(f32[8,16,12,512]{3,1,2,0:T(8,128)} %bitcast.8) | data formatting | bytes 6291456
  118.0 0.0 copy-done
  118.0 0.0 copy-start.1
  118.0 1.7 %copy.12 = f32[8,16,12,512]{3,1,2,0:T(8,128)} copy(f32[8,16,12,512]{3,1,2,0:T(8,128)S(1)} %bitcast.7) | data formatting | bytes 6291456
  119.6 0.0 copy-done.1
  119.6 0.8 copy.13
Async XLA Ops:
  113.7 4.3 %copy-start = (f32[8,12,16,512]{3,2,1,0:T(8,128)S(1)}, f32[8,12,16,512]{3,2,1,0:T(8,128)}, u32[]{:S(2)}) copy-start(f32[8,12,16,512]{3,2,1,0:T(8,128)} %get-tuple-element.7) | copy-start | bytes 9437188
  118.0 1.7 %copy-start.1 = (f32[512,256]{1,0:T(8,128)S(1)}, f32[512,256]{1,0:T(8,128)}, u32[]{:S(2)}) copy-start(f32[512,256]{1,0:T(8,128)} %get-tuple-element.14) | copy-start | bytes 1572868
